TPU v7x, 512 devices: a whole 4x4x16 slice. The times are simulated.
512 devices in a mesh: tile: 64 (over y_lo, z, core), dgrp: 8 (over y_hi, x).
Axes of the slice: x: 4, y: 4 (y_hi: 2, y_lo: 2; y = y_hi * 2 + y_lo), z: 16, core: 2. Of those that a mesh axis runs over, the one named last changes fastest.
Arguments:
- prediction_state: bfloat16 [8, 512, 1024], P(None, 'tile'), may hold values from -6 to 6
- hindcast_store: bfloat16 [64, 8, 512, 1024], P('dgrp', None, 'tile'), may hold values from -6 to 6
- verifying_truth: bfloat16 [64, 512, 1024], P('dgrp', 'tile'), may hold values from -6 to 6
- quantity_factor: float32 [8], replicated, may hold values from 0.03 to 0.4
- tile_day_choices: int32 [64, 48], replicated, may hold values from 0 to 63, as said below
- filled_lengths: int32 [64], replicated, may hold values from 16 to 48
Outputs:
- analog: float32 [512, 1024], P('dgrp', 'tile')
Inputs may be any that keep to these rules, and one draw needn't show every extreme that they name: `tile_day_choices`: each row holds distinct dates; only the first filled_lengths entries of a row are used.
All inputs are finite; a program needn't handle non-finite values.
Results may differ from a plain program's by a relative error of at most 0.00035.
Values may be sent and summed in bfloat16 or wider, within the bound.
No kernel may reach another device: no remote copies, remote signals or barrier semaphores. Data moves between devices by JAX's collectives and lax.ppermute only.
A program may use at most 64 MiB of HBM per device.

v0:
```python
import jax
import jax.numpy as jnp
from jax import lax
from jax.sharding import PartitionSpec as P


def with_halo(cells, sides, width):
    for axis, dim in sides:
        count = lax.axis_size(axis)
        ends = count - 1
        head = lax.slice_in_dim(cells, 0, width, axis=dim)
        tail = lax.slice_in_dim(cells, cells.shape[dim] - width, cells.shape[dim], axis=dim)
        cells = jnp.concatenate(
            [
                lax.ppermute(tail, axis, [(i, (i + 1) % count) for i in range(ends)]),
                cells,
                lax.ppermute(head, axis, [((i + 1) % count, i) for i in range(ends)]),
            ],
            axis=dim,
        )
    return cells


def member_table(tile_day_choices, filled_lengths, dates):
    hit = tile_day_choices[:, :, None] == dates[None, None, :]
    live = (
        jnp.arange(tile_day_choices.shape[1], dtype=jnp.int32)[None, :, None]
        < filled_lengths[:, None, None]
    )
    return jnp.any(hit & live, axis=1).astype(jnp.float32)


def box_sum(padded):
    rows_sum = padded[..., :-2, :] + padded[..., 1:-1, :] + padded[..., 2:, :]
    return rows_sum[..., :-2] + rows_sum[..., 1:-1] + rows_sum[..., 2:]


def mismatch_totals(predicted_quantity, hindcast_reserve, quantity_factor):
    deviation = predicted_quantity.astype(jnp.float32)[None] - hindcast_reserve.astype(jnp.float32)
    return jnp.sum(quantity_factor[None, :, None, None] * deviation * deviation, axis=1)


def weights_of(err_padded):
    dist = box_sum(err_padded) / 9.0
    base = 1.0 / (1.0 + dist)
    squared_deviation = base * base
    return squared_deviation * squared_deviation


def local(
    prediction_state,
    hindcast_store,
    verifying_truth,
    quantity_factor,
    tile_day_choices,
    filled_lengths,
):
    days_in_batch, quantity_total = (hindcast_store.shape[0], hindcast_store.shape[1])
    mesh_lines, neighbourhood_span = (prediction_state.shape[1], prediction_state.shape[2])
    dates = lax.axis_index("dgrp") * days_in_batch + jnp.arange(days_in_batch, dtype=jnp.int32)
    member = member_table(tile_day_choices, filled_lengths, dates)
    input_arrays = jnp.concatenate(
        [
            prediction_state,
            hindcast_store.reshape(days_in_batch * quantity_total, mesh_lines, neighbourhood_span),
        ],
        0,
    )
    grown = with_halo(input_arrays, (("tile", 1),), 1)
    grown = jnp.pad(grown, ((0, 0), (0, 0), (1, 1)))
    hindcast_reserve = grown[quantity_total:].reshape(
        days_in_batch, quantity_total, mesh_lines + 2, neighbourhood_span + 2
    )
    err = mismatch_totals(grown[:quantity_total], hindcast_reserve, quantity_factor)
    tile_width = neighbourhood_span // lax.axis_size("tile")
    live = jnp.repeat(jnp.transpose(member), tile_width, axis=1)
    weight = weights_of(err) * live[:, None, :]
    band_num = jnp.sum(weight * verifying_truth.astype(jnp.float32), axis=0)
    band_den = jnp.sum(weight, axis=0)
    num, den = (
        lax.all_to_all(band_num, "tile", split_axis=1, concat_axis=0, tiled=True),
        lax.all_to_all(band_den, "tile", split_axis=1, concat_axis=0, tiled=True),
    )
    num, den = (
        lax.psum_scatter(num, "dgrp", scatter_dimension=0, tiled=True),
        lax.psum_scatter(den, "dgrp", scatter_dimension=0, tiled=True),
    )
    return num / den


def solution(mesh):
    in_specs = (
        P(None, "tile", None),
        P("dgrp", None, "tile", None),
        P("dgrp", "tile", None),
        P(),
        P(),
        P(),
    )
    out_specs = P("dgrp", "tile")
    return jax.shard_map(local, mesh=mesh, in_specs=in_specs, out_specs=out_specs, check_vma=False)
```

profile of v0, /device:TPU:1, one launch (start us, length us, event | category | flops | bytes accessed | tf_op | source)
XLA Modules:
  0.0 251.7 jit_solution(5055787572031532335)
XLA Ops:
  6.5 0.0 copy-start
  6.5 2.2 pad_maximum_fusion.1
  8.7 4.9 %collective-permute-start = (bf16[72,1,1024]{2,1,0:T(2,128)(2,1)S(1)}, bf16[72,1,1024]{2,1,0:T(2,128)(2,1)S(1)}, u32[]{:S(2)}, u32[]{:S(2)}) collective-permute-start(bf16[72,1,1024]{2,1,0:T(2,128)(2,1)S(1)} %get-tuple-element.7), channel_id=1, source_target_pairs={{0,8},{8,16},{16,24},{24,32},{32,40},{40,48},{48,56},{56,64},{64,7... | collective-permute-start | bytes 442376 | tf_op jit(solution)/shard_map/ppermute | solution.py:15
  13.7 5.2 %collective-permute-start.1 = (bf16[72,1,1024]{2,1,0:T(2,128)(2,1)S(1)}, bf16[72,1,1024]{2,1,0:T(2,128)(2,1)S(1)}, u32[]{:S(2)}, u32[]{:S(2)}) collective-permute-start(bf16[72,1,1024]{2,1,0:T(2,128)(2,1)S(1)} %get-tuple-element.8), channel_id=1, source_target_pairs={{8,0},{16,8},{24,16},{32,24},{40,32},{48,40},{56,48},{64,56},{72,6... | collective-permute-start | bytes 442376 | tf_op jit(solution)/shard_map/ppermute | solution.py:17
  18.9 0.7 iota_compare_fusion.2
  19.5 0.9 and_reduce_fusion
  20.4 0.1 broadcast_in_dim.2
  20.5 0.2 mul.39
  20.7 0.0 copy-start.2
  20.7 0.0 collective-permute-done
  20.7 1.0 collective-permute-done.1
  21.7 0.0 copy-done
  21.7 5.4 %select_maximum_fusion = bf16[72,10,1026]{2,1,0:T(8,128)(2,1)S(1)} fusion(bf16[72,1,1024]{2,1,0:T(2,128)(2,1)S(1)} %collective-permute-done.1, bf16[72,1,1024]{2,1,0:T(2,128)(2,1)S(1)} %collective-permute-done, bf16[64,8,1024]{2,1,0:T(8,128)(2,1)S(1)} %bitcast.25, bf16[8,8,1024]{2,1,0:T(8,128)(2,1)} %param.6), kind=kLoop, calls=%fused_computation.6 | loop fusion | flops 11080800 | bytes 2952000 | tf_op jit(solution)/shard_map/concatenate | solution.py:13
  27.1 0.0 copy-start.1
  27.2 0.0 copy-done.2
  27.2 0.9 fusion.1
  28.1 0.1 slice_add_fusion
  28.2 0.0 copy-done.1
  28.2 0.2 fusion.11
  28.4 0.1 all_to_all.28
  28.5 0.2 copy.22
  28.7 0.8 reshape.47
  29.4 16.6 %all-to-all-start = ((f32[64,1,128]{2,1,0:T(1,128)}), f32[64,1,128]{2,1,0:T(1,128)S(1)}, u32[]{:S(2)}, u32[]{:S(2)}) async-start(f32[64,1,128]{2,1,0:T(1,128)} %reshape.47), calls=%async_computation | async-start | bytes 65536 | tf_op jit(solution)/shard_map/all_to_all | solution.py:81
  46.1 0.1 all_to_all.32
  46.2 0.2 copy.21
  46.4 0.7 reshape.49
  47.1 12.2 %all-to-all-done = f32[64,1,128]{2,1,0:T(1,128)S(1)} async-done(((f32[64,1,128]{2,1,0:T(1,128)}), f32[64,1,128]{2,1,0:T(1,128)S(1)}, u32[]{:S(2)}, u32[]{:S(2)}) %all-to-all-start) | async-done | bytes 32800 | tf_op jit(solution)/shard_map/all_to_all | solution.py:81
  59.3 4.6 %all-to-all-start.1 = ((f32[64,1,128]{2,1,0:T(1,128)}), f32[64,1,128]{2,1,0:T(1,128)S(1)}, u32[]{:S(2)}, u32[]{:S(2)}) async-start(f32[64,1,128]{2,1,0:T(1,128)} %reshape.49), calls=%async_computation.2 | async-start | bytes 65536 | tf_op jit(solution)/shard_map/all_to_all | solution.py:82
  64.0 0.0 reduce-scatter.3.cloned.1.call-start
  64.0 0.5 broadcast.48
  64.5 0.7 reduce
  65.3 0.1 reshape.48
  65.4 0.7 bitcast_bitcast_fusion.1
  66.1 0.0 reduce-scatter.3.cloned.1.call-update
  66.1 0.0 reduce-scatter.5.cloned.1.call-start
  66.2 11.2 %all-to-all-done.1 = f32[64,1,128]{2,1,0:T(1,128)S(1)} async-done(((f32[64,1,128]{2,1,0:T(1,128)}), f32[64,1,128]{2,1,0:T(1,128)S(1)}, u32[]{:S(2)}, u32[]{:S(2)}) %all-to-all-start.1) | async-done | bytes 32800 | tf_op jit(solution)/shard_map/all_to_all | solution.py:82
  77.3 0.7 reduce.1
  78.1 0.1 reshape.50
  78.2 0.7 bitcast_bitcast_fusion
  78.9 0.0 reduce-scatter.5.cloned.1.call-update
  78.9 74.7 %reduce-scatter.3.cloned.1.call-done = f32[64,16]{1,0:T(8,128)} async-done(((f32[512,16]{1,0:T(8,128)}), f32[64,16]{1,0:T(8,128)}) %reduce-scatter.3.cloned.1.call-update) | async-done | bytes 4112 | tf_op jit(solution)/shard_map/reduce_scatter | solution.py:85
  153.6 89.7 %reduce-scatter.5.cloned.1.call-done = f32[64,16]{1,0:T(8,128)} async-done(((f32[512,16]{1,0:T(8,128)}), f32[64,16]{1,0:T(8,128)}) %reduce-scatter.5.cloned.1.call-update) | async-done | bytes 4112 | tf_op jit(solution)/shard_map/reduce_scatter | solution.py:86
  243.4 0.8 div.15
  244.2 0.7 copy.18
  (3 shorter events, 0.1 us)
Async XLA Ops:
  6.5 15.2 %copy-start = (bf16[8,8,8,1024]{3,2,1,0:T(8,128)(2,1)S(1)}, bf16[8,8,8,1024]{3,2,1,0:T(8,128)(2,1)}, u32[]{:S(2)}) copy-start(bf16[8,8,8,1024]{3,2,1,0:T(8,128)(2,1)} %param.7) | copy-start | bytes 3145732
  8.7 12.0 %collective-permute-start = (bf16[72,1,1024]{2,1,0:T(2,128)(2,1)S(1)}, bf16[72,1,1024]{2,1,0:T(2,128)(2,1)S(1)}, u32[]{:S(2)}, u32[]{:S(2)}) collective-permute-start(bf16[72,1,1024]{2,1,0:T(2,128)(2,1)S(1)} %get-tuple-element.7), channel_id=1, source_target_pairs={{0,8},{8,16},{16,24},{24,32},{32,40},{40,48},{48,56},{56,64},{64,7... | collective-permute-start | bytes 442376 | tf_op jit(solution)/shard_map/ppermute | solution.py:15
  13.7 8.0 %collective-permute-start.1 = (bf16[72,1,1024]{2,1,0:T(2,128)(2,1)S(1)}, bf16[72,1,1024]{2,1,0:T(2,128)(2,1)S(1)}, u32[]{:S(2)}, u32[]{:S(2)}) collective-permute-start(bf16[72,1,1024]{2,1,0:T(2,128)(2,1)S(1)} %get-tuple-element.8), channel_id=1, source_target_pairs={{8,0},{16,8},{24,16},{32,24},{40,32},{48,40},{56,48},{64,56},{72,6... | collective-permute-start | bytes 442376 | tf_op jit(solution)/shard_map/ppermute | solution.py:17
  20.7 6.5 %copy-start.2 = (f32[8]{0:T(128)S(1)}, f32[8]{0:T(128)}, u32[]{:S(2)}) copy-start(f32[8]{0:T(128)} %param.9) | copy-start | bytes 100
  27.1 1.1 copy-start.1
  29.4 29.9 %all-to-all-start = ((f32[64,1,128]{2,1,0:T(1,128)}), f32[64,1,128]{2,1,0:T(1,128)S(1)}, u32[]{:S(2)}, u32[]{:S(2)}) async-start(f32[64,1,128]{2,1,0:T(1,128)} %reshape.47), calls=%async_computation | async-start | bytes 65536 | tf_op jit(solution)/shard_map/all_to_all | solution.py:81
  59.3 18.0 %all-to-all-start.1 = ((f32[64,1,128]{2,1,0:T(1,128)}), f32[64,1,128]{2,1,0:T(1,128)S(1)}, u32[]{:S(2)}, u32[]{:S(2)}) async-start(f32[64,1,128]{2,1,0:T(1,128)} %reshape.49), calls=%async_computation.2 | async-start | bytes 65536 | tf_op jit(solution)/shard_map/all_to_all | solution.py:82
  64.0 89.7 %reduce-scatter.3.cloned.1.call-start = ((), (), s32[]{:S(2)}) async-start(), calls=%async_computation.4 | async-start | bytes 294912 | tf_op jit(solution)/shard_map/reduce_scatter | solution.py:85
  66.1 177.2 %reduce-scatter.5.cloned.1.call-start = ((), (), s32[]{:S(2)}) async-start(), calls=%async_computation.5 | async-start | bytes 294912 | tf_op jit(solution)/shard_map/reduce_scatter | solution.py:86
Sparse Core Ops, SparseCore 0:
  69.2 84.3 reduce-scatter.2
  158.7 84.6 reduce-scatter.4
where the time goes:
time: 253 us; the launch traced here: 252 us
  waiting for transfers between devices  189 us (75%)
  starting transfers between devices  31.4 us (12%)
  between operations  13.6 us (5%)
  other arithmetic  12.6 us (5%)
  local copies, waits for them, and re-layouts  5.21 us (2%)
    reduce_scatter x1, waiting for transfers between devices, local(): lax.psum_scatter(den, 'dgrp', scatter_dimension=0, tiled=True)  89.7 us
    reduce_scatter x1, waiting for transfers between devices, local(): lax.psum_scatter(num, 'dgrp', scatter_dimension=0, tiled=True)  74.7 us
    all_to_all x1, starting transfers between devices, local(): lax.all_to_all(band_num, 'tile', split_axis=1, concat_axis=0, tiled=True)  16.6 us
    all_to_all x1, waiting for transfers between devices, local(): lax.all_to_all(band_num, 'tile', split_axis=1, concat_axis=0, tiled=True)  12.2 us
    all_to_all x1, waiting for transfers between devices, local(): lax.all_to_all(band_den, 'tile', split_axis=1, concat_axis=0, tiled=True)  11.2 us
    concatenate x1, other arithmetic, with_halo(): jnp.concatenate([lax.ppermute(tail, axis, [(i, (i + 1) % count) for i in...  5.35 us
    ppermute x1, starting transfers between devices, with_halo(): lax.ppermute(head, axis, [((i + 1) % count, i) for i in range(ends)])  5.16 us
  transfers between devices with their start and end apart: 6, of which 5 were waited for; matrix products, arithmetic and copies ran while one was open for 3% of the time, Pallas kernels for 0%

commit v1 on v0

v1 whole, which is shorter than its diff:
```python
import functools

import jax
import jax.numpy as jnp
from jax import lax
from jax.experimental import pallas as pl
from jax.experimental.pallas import tpu as pltpu
from jax.sharding import PartitionSpec as P

DATES, QTYS, ROWS, COLS = 8, 8, 8, 1024
TILES, TW, LANES = 64, 16, 128
MAXC = 48
GROUPS = LANES // TW


def member_rows(base, choices, filled):
    slot = lax.broadcasted_iota(jnp.int32, (MAXC, TILES), 0)
    local = jnp.where(slot < filled, choices - base, -1)
    flags = [
        jnp.sum(jnp.where(local == d, 1.0, 0.0), axis=0, keepdims=True) for d in range(DATES)
    ]
    flags = jnp.concatenate(flags, axis=0).astype(jnp.bfloat16)
    tile = lax.broadcasted_iota(jnp.int32, (TILES, COLS), 0)
    col = lax.broadcasted_iota(jnp.int32, (TILES, COLS), 1)
    spread = jnp.where(col // TW == tile, 1.0, 0.0).astype(jnp.bfloat16)
    return jnp.dot(flags, spread, preferred_element_type=jnp.float32)


def fourth(dist9):
    base = 1.0 / (1.0 + dist9 / 9.0)
    base = base * base
    return base * base


def band_kernel(
    first_date, factor, pred, hind, truth, choices, filled, out, held, shown, exact, parts, sems
):
    copies = [pltpu.make_async_copy(hind.at[d], held.at[d], sems.at[d]) for d in range(DATES)]
    seen = pltpu.make_async_copy(pred, shown, sems.at[DATES])
    seen.start()
    for copy in copies:
        copy.start()
    member = member_rows(first_date(), choices[...], filled[...])
    col = lax.broadcasted_iota(jnp.int32, (ROWS, COLS), 1)
    sub = lax.broadcasted_iota(jnp.int32, (ROWS, COLS), 0)
    seen.wait()
    exact[...] = shown[...].astype(jnp.float32)
    num = jnp.zeros((ROWS, COLS), jnp.float32)
    den = jnp.zeros((ROWS, COLS), jnp.float32)
    for d in range(DATES):
        copies[d].wait()
        err = jnp.zeros((ROWS, COLS), jnp.float32)
        for v in range(QTYS):
            dev = exact[v] - held[d, v].astype(jnp.float32)
            err = err + factor[v] * dev * dev
        left = jnp.where(col == 0, 0.0, pltpu.roll(err, 1, 1))
        right = jnp.where(col == COLS - 1, 0.0, pltpu.roll(err, COLS - 1, 1))
        side = err + left + right
        above, below = pltpu.roll(side, 1, 0), pltpu.roll(side, ROWS - 1, 0)
        flag = jnp.broadcast_to(member[d : d + 1], (ROWS, COLS))
        seen_truth = truth[d].astype(jnp.float32)
        weight = fourth(side + above + below) * flag
        num = num + weight * seen_truth
        den = den + weight
        part = jnp.where(sub == 1, jnp.where(flag > 0, side + above, -1.0), side)
        part = jnp.where(sub == 6, jnp.where(flag > 0, side + below, -1.0), part)
        part = jnp.where(sub == 2, pltpu.roll(seen_truth, 2, 0), part)
        part = jnp.where(sub == 5, pltpu.roll(seen_truth, ROWS - 2, 0), part)
        parts[d] = part
    lane = lax.broadcasted_iota(jnp.int32, (ROWS, LANES), 1) // TW
    sub = lax.broadcasted_iota(jnp.int32, (ROWS, LANES), 0)
    for j in range(COLS // LANES):
        at = slice(j * LANES, (j + 1) * LANES)
        v = []
        for d in range(DATES):
            part = parts[d, :, at]
            part = jnp.where(sub == 3, pltpu.roll(num[:, at], (3 - d) % ROWS, 0), part)
            part = jnp.where(sub == 4, pltpu.roll(den[:, at], (4 - d) % ROWS, 0), part)
            v.append(part)
        for s in (1, 2, 4):
            odd = (lane & s) != 0
            for a in range(GROUPS):
                if a & s:
                    continue
                low, high = v[a], v[a | s]
                v[a] = jnp.where(odd, pltpu.roll(high, TW * s, 1), low)
                v[a | s] = jnp.where(odd, high, pltpu.roll(low, LANES - TW * s, 1))
        for t in range(GROUPS):
            out[j * GROUPS + t] = v[t]


def band_blocks(first_date, prediction, hindcast, truth, factor, choices, filled, **kw):
    vmem = pl.BlockSpec(memory_space=pltpu.VMEM)
    hbm = pl.BlockSpec(memory_space=pl.ANY)
    return pl.pallas_call(
        functools.partial(band_kernel, first_date),
        out_shape=jax.ShapeDtypeStruct((TILES, ROWS, LANES), jnp.float32),
        in_specs=[pl.BlockSpec(memory_space=pltpu.SMEM), hbm, hbm, vmem, vmem, vmem],
        out_specs=vmem,
        scratch_shapes=[
            pltpu.VMEM((DATES, QTYS, ROWS, COLS), jnp.bfloat16),
            pltpu.VMEM((QTYS, ROWS, COLS), jnp.bfloat16),
            pltpu.VMEM((QTYS, ROWS, COLS), jnp.float32),
            pltpu.VMEM((DATES, ROWS, COLS), jnp.float32),
            pltpu.SemaphoreType.DMA((DATES + 1,)),
        ],
        compiler_params=pltpu.CompilerParams(vmem_limit_bytes=16 << 20),
        **kw,
    )(factor, prediction, hindcast, truth, choices.T, filled[None])


def lane_groups_sum(x):
    for s in (4, 2, 1):
        x = x + pltpu.roll(x, TW * s, 1)
    return x


def column_kernel(got, out):
    side0, pair0, truth0, num = got[:, 0], got[:, 1], got[:, 2], got[:, 3]
    den, truth7, pair7, side7 = got[:, 4], got[:, 5], got[:, 6], got[:, 7]
    band = lax.broadcasted_iota(jnp.int32, (TILES, LANES), 0)
    row = lax.broadcasted_iota(jnp.int32, (TILES, LANES), 1) // TW
    above = jnp.where(band == 0, 0.0, pltpu.roll(side7, 1, 0))
    below = jnp.where(band == TILES - 1, 0.0, pltpu.roll(side0, TILES - 1, 0))
    weight0 = jnp.where(pair0 < 0, 0.0, fourth(pair0 + above))
    weight7 = jnp.where(pair7 < 0, 0.0, fourth(pair7 + below))
    num = jnp.where(row == 0, lane_groups_sum(weight0 * truth0), num)
    num = jnp.where(row == ROWS - 1, lane_groups_sum(weight7 * truth7), num)
    den = jnp.where(row == 0, lane_groups_sum(weight0), den)
    den = jnp.where(row == ROWS - 1, lane_groups_sum(weight7), den)
    for g in range(8):
        out[g, 0:8] = num[8 * g : 8 * g + 8]
        out[g, 8:16] = den[8 * g : 8 * g + 8]


def column_sums(got, **kw):
    vmem = pl.BlockSpec(memory_space=pltpu.VMEM)
    return pl.pallas_call(
        column_kernel,
        out_shape=jax.ShapeDtypeStruct((8, 16, LANES), jnp.float32),
        in_specs=[vmem],
        out_specs=vmem,
        **kw,
    )(got)


def analog_kernel(sums, out):
    total = sums[0]
    for g in range(1, 8):
        total = total + sums[g]
    analog = total[0:8] / total[8:16]
    lane = lax.broadcasted_iota(jnp.int32, (8, LANES), 1)
    sub = lax.broadcasted_iota(jnp.int32, (8, LANES), 0)
    x = jnp.take_along_axis(analog, (lane % 8) * TW + lane // 8, axis=1)
    for s in (1, 2, 4):
        odd_lane, odd_sub = ((lane // 8) & s) != 0, (sub & s) != 0
        up = pltpu.roll(pltpu.roll(x, 8 - s, 0), 8 * s, 1)
        down = pltpu.roll(pltpu.roll(x, s, 0), LANES - 8 * s, 1)
        x = jnp.where(odd_lane == odd_sub, x, jnp.where(odd_lane, up, down))
    out[0:8] = x[:, 0:64]
    out[8:16] = x[:, 64:128]


def analog_block(sums, **kw):
    vmem = pl.BlockSpec(memory_space=pltpu.VMEM)
    return pl.pallas_call(
        analog_kernel,
        out_shape=jax.ShapeDtypeStruct((TW, 64), jnp.float32),
        in_specs=[vmem],
        out_specs=vmem,
        **kw,
    )(sums)


def local(
    prediction_state,
    hindcast_store,
    verifying_truth,
    quantity_factor,
    tile_day_choices,
    filled_lengths,
):
    blocks = band_blocks(
        lambda: lax.axis_index("dgrp") * DATES,
        prediction_state,
        hindcast_store,
        verifying_truth,
        quantity_factor,
        tile_day_choices,
        filled_lengths,
    )
    got = lax.all_to_all(blocks, "tile", split_axis=0, concat_axis=0, tiled=True)
    sums = column_sums(got)
    sums = lax.all_to_all(sums, "dgrp", split_axis=0, concat_axis=0, tiled=True)
    return analog_block(sums).T


def solution(mesh):
    in_specs = (
        P(None, "tile", None),
        P("dgrp", None, "tile", None),
        P("dgrp", "tile", None),
        P(),
        P(),
        P(),
    )
    out_specs = P("dgrp", "tile")
    return jax.shard_map(local, mesh=mesh, in_specs=in_specs, out_specs=out_specs, check_vma=False)
```

time: 253 us -> 66 us (0.26)
  waiting for transfers between devices: 189 us -> 0 us
  blocking collectives: 0 us -> 53.5 us
  starting transfers between devices: 31.4 us -> 0 us
  between operations: 13.6 us -> 0.02 us
  other arithmetic: 12.6 us -> 0 us
  Pallas kernels: 0 us -> 7.65 us
    reduce_scatter x2 -> x0, waiting for transfers between devices: 164 us -> none  [the longest x1 89.7 us: local(): lax.psum_scatter(den, 'dgrp', scatter_dimension=0, tiled=True)]
    all_to_all x0 -> x2, blocking collectives: none -> 53.5 us  [the longest x1 40.3 us: local(): lax.all_to_all(blocks, 'tile', split_axis=0, concat_axis=0, tiled=True)]
    all_to_all x2 -> x0, waiting for transfers between devices: 23.4 us -> none  [the longest x1 12.2 us: local(): lax.all_to_all(band_num, 'tile', split_axis=1, concat_axis=0, tiled=True)]
    all_to_all x2 -> x0, starting transfers between devices: 21.3 us -> none  [the longest x1 16.6 us: local(): lax.all_to_all(band_num, 'tile', split_axis=1, concat_axis=0, tiled=True)]
    ppermute x2 -> x0, starting transfers between devices: 10.1 us -> none  [the longest x1 5.16 us: with_halo(): lax.ppermute(head, axis, [((i + 1) % count, i) for i in range(ends)])]
    pallas_call x0 -> x3, Pallas kernels: none -> 7.65 us  [the longest x1 3.86 us: band_blocks(): pl.pallas_call(functools.partial(band_kernel, first_date), out_shape=jax....]
    concatenate x1 -> x0, other arithmetic: 5.35 us -> none  [with_halo(): jnp.concatenate([lax.ppermute(tail, axis, [(i, (i + 1) % count) for i in...]
    unnamed x10 -> x12, local copies, waits for them, and re-layouts: 1.76 us -> 4.44 us
  transfers between devices with their start and end apart: 6 -> 0, of which waited for: 5 -> 0; matrix products, arithmetic and copies ran while one was open for 3% -> 0% of each run, Pallas kernels for 0% -> 0%
where the time goes in v1:
time: 66 us; the launch traced here: 65.6 us
  blocking collectives  53.5 us (81%)
  Pallas kernels  7.65 us (12%)
  local copies, waits for them, and re-layouts  4.44 us (7%)
    all_to_all x1, blocking collectives, local(): lax.all_to_all(blocks, 'tile', split_axis=0, concat_axis=0, tiled=True)  40.3 us
    all_to_all x1, blocking collectives, local(): sums = lax.all_to_all(sums, 'dgrp', split_axis=0, concat_axis=0, tiled=True)  13.2 us
    unnamed x12, local copies, waits for them, and re-layouts  4.44 us
    pallas_call x1, Pallas kernels, band_blocks(): pl.pallas_call(functools.partial(band_kernel, first_date), out_shape=jax....  3.86 us
    pallas_call x1, Pallas kernels, column_sums(): pl.pallas_call(column_kernel, out_shape=jax.ShapeDtypeStruct((8, 16, LANE...  1.99 us
    pallas_call x1, Pallas kernels, analog_block(): pl.pallas_call(analog_kernel, out_shape=jax.ShapeDtypeStruct((TW, 64), jn...  1.8 us

profile of v1, /device:TPU:1, one launch (start us, length us, event | category | flops | bytes accessed | tf_op | source)
XLA Modules:
  0.0 65.6 jit_solution(16993084053096298169)
XLA Ops:
  0.0 0.0 copy-start.4
  0.0 0.0 copy-start.5
  0.0 0.7 copy-done.4
  0.7 0.0 copy-done.5
  0.7 0.0 copy-start
  0.7 1.2 %copy-done = bf16[8,8,8,1024]{3,2,1,0:T(8,128)(2,1)S(1)} copy-done((bf16[8,8,8,1024]{3,2,1,0:T(8,128)(2,1)S(1)}, bf16[8,8,8,1024]{3,2,1,0:T(8,128)(2,1)}, u32[]{:S(2)}) %copy-start) | copy-done | bytes 1048600
  1.9 0.0 copy-start.1
  1.9 0.9 %copy-done.1 = bf16[8,8,1024]{2,1,0:T(8,128)(2,1)S(1)} copy-done((bf16[8,8,1024]{2,1,0:T(8,128)(2,1)S(1)}, bf16[8,8,1024]{2,1,0:T(8,128)(2,1)}, u32[]{:S(2)}) %copy-start.1) | copy-done | bytes 131096
  2.8 0.0 copy-start.2
  2.8 0.9 %copy-done.2 = bf16[8,8,1024]{2,1,0:T(8,128)(2,1)S(1)} copy-done((bf16[8,8,1024]{2,1,0:T(8,128)(2,1)S(1)}, bf16[8,8,1024]{2,1,0:T(8,128)(2,1)}, u32[]{:S(2)}) %copy-start.2) | copy-done | bytes 131096
  3.7 0.0 copy-start.3
  3.7 0.7 %copy-done.3 = s32[64,48]{0,1:T(8,128)S(1)} copy-done((s32[64,48]{0,1:T(8,128)S(1)}, s32[64,48]{0,1:T(8,128)}, u32[]{:S(2)}) %copy-start.3) | copy-done | bytes 12312
  4.4 3.9 %shard_map.64 = f32[64,8,128]{2,1,0:T(8,128)S(1)} custom-call(f32[8]{0:T(128)S(1)} %copy-done.4, bf16[8,8,1024]{2,1,0:T(8,128)(2,1)S(1)} %copy-done.1, bf16[8,8,8,1024]{3,2,1,0:T(8,128)(2,1)S(1)} %copy-done, bf16[8,8,1024]{2,1,0:T(8,128)(2,1)S(1)} %copy-done.2, s32[48,64]{1,0:T(8,128)S(1)} %bitcast.3, s32[1,64]{1,0:T(1,128)S(1)} %bitcast.4), custom_call_target="tpu_custom_call" | custom-call | tf_op jit(solution)/shard_map/pallas_call | solution.py:95
  8.3 40.3 %all_to_all.10.got = f32[64,8,128]{2,1,0:T(8,128)} all-to-all(f32[64,8,128]{2,1,0:T(8,128)S(1)} %shard_map.64), channel_id=1, replica_groups=mesh['tile'=64,'dgrp'=8] {'tile'}, dimensions={0} | all-to-all | bytes 524288 | tf_op jit(solution)/shard_map/all_to_all | solution.py:192
  48.6 2.0 %shard_map.65 = f32[8,16,128]{2,1,0:T(8,128)} custom-call(f32[64,8,128]{2,1,0:T(8,128)} %all_to_all.10.got), custom_call_target="tpu_custom_call" | custom-call | tf_op jit(solution)/shard_map/pallas_call | solution.py:138
  50.6 13.2 %all_to_all.11.sums = f32[8,16,128]{2,1,0:T(8,128)} all-to-all(f32[8,16,128]{2,1,0:T(8,128)} %shard_map.65), channel_id=1, replica_groups=mesh['tile'=64,'dgrp'=8] {'dgrp'}, dimensions={0} | all-to-all | bytes 131072 | tf_op jit(solution)/shard_map/all_to_all | solution.py:194
  63.8 1.8 %shard_map.66 = f32[16,64]{1,0:T(8,128)} custom-call(f32[8,16,128]{2,1,0:T(8,128)} %all_to_all.11.sums), custom_call_target="tpu_custom_call" | custom-call | tf_op jit(solution)/shard_map/pallas_call | solution.py:166
Async XLA Ops:
  0.0 0.7 copy-start.4
  0.0 0.7 %copy-start.5 = (s32[64]{0:T(128)S(1)}, s32[64]{0:T(128)}, u32[]{:S(2)}) copy-start(s32[64]{0:T(128)} %param.11) | copy-start | bytes 772
  0.7 1.2 %copy-start = (bf16[8,8,8,1024]{3,2,1,0:T(8,128)(2,1)S(1)}, bf16[8,8,8,1024]{3,2,1,0:T(8,128)(2,1)}, u32[]{:S(2)}) copy-start(bf16[8,8,8,1024]{3,2,1,0:T(8,128)(2,1)} %hind.1) | copy-start | bytes 3145732
  1.9 0.9 %copy-start.1 = (bf16[8,8,1024]{2,1,0:T(8,128)(2,1)S(1)}, bf16[8,8,1024]{2,1,0:T(8,128)(2,1)}, u32[]{:S(2)}) copy-start(bf16[8,8,1024]{2,1,0:T(8,128)(2,1)} %pred_.1) | copy-start | bytes 393220
  2.8 0.9 %copy-start.2 = (bf16[8,8,1024]{2,1,0:T(8,128)(2,1)S(1)}, bf16[8,8,1024]{2,1,0:T(8,128)(2,1)}, u32[]{:S(2)}) copy-start(bf16[8,8,1024]{2,1,0:T(8,128)(2,1)} %truth.1) | copy-start | bytes 393220
  3.7 0.7 %copy-start.3 = (s32[64,48]{0,1:T(8,128)S(1)}, s32[64,48]{0,1:T(8,128)}, u32[]{:S(2)}) copy-start(s32[64,48]{0,1:T(8,128)} %param.10) | copy-start | bytes 36868

commit v2 on v1

--- a/solution.py
+++ b/solution.py
@@ -11,6 +11,9 @@
 TILES, TW, LANES = 64, 16, 128
 MAXC = 48
 GROUPS = LANES // TW
+
+SQUARE_SCALE, MEAN_SCALE, TRUTH_SCALE = 2.0**-7, 2.0**10, 2.0**13
+SMALL, LARGE_SCALE, SMALL_SCALE = 2.0**-26, 2.0**12, 2.0**41
 
 
 def member_rows(base, choices, filled):
@@ -30,6 +33,11 @@
     base = 1.0 / (1.0 + dist9 / 9.0)
     base = base * base
     return base * base
+
+
+def to_11_bits(x):
+    c = x * (2.0**13 + 1)
+    return c - (c - x)
 
 
 def band_kernel(
@@ -62,11 +70,17 @@
         weight = fourth(side + above + below) * flag
         num = num + weight * seen_truth
         den = den + weight
-        part = jnp.where(sub == 1, jnp.where(flag > 0, side + above, -1.0), side)
-        part = jnp.where(sub == 6, jnp.where(flag > 0, side + below, -1.0), part)
-        part = jnp.where(sub == 2, pltpu.roll(seen_truth, 2, 0), part)
-        part = jnp.where(sub == 5, pltpu.roll(seen_truth, ROWS - 2, 0), part)
-        parts[d] = part
+        pair = jnp.where(sub == 1, side + above, side + below)
+        pair = jnp.where(flag > 0, pair * pair * SQUARE_SCALE, -1.0)
+        part = jnp.where((sub == 1) | (sub == 6), pair, side * side * SQUARE_SCALE)
+        scaled = seen_truth * TRUTH_SCALE
+        part = jnp.where(sub == 2, pltpu.roll(scaled, 2, 0), part)
+        parts[d] = jnp.where(sub == 5, pltpu.roll(scaled, ROWS - 2, 0), part)
+    high = den >= SMALL
+    den = to_11_bits(jnp.where(high, den * LARGE_SCALE, den * -SMALL_SCALE))
+    held_den = jnp.where(high, den * (1 / LARGE_SCALE), den * (-1 / SMALL_SCALE))
+    mean = jnp.where(held_den > 0, num / held_den, 0.0)
+    num = mean * jnp.abs(mean) * MEAN_SCALE
     lane = lax.broadcasted_iota(jnp.int32, (ROWS, LANES), 1) // TW
     sub = lax.broadcasted_iota(jnp.int32, (ROWS, LANES), 0)
     for j in range(COLS // LANES):
@@ -104,9 +118,14 @@
             pltpu.VMEM((DATES, ROWS, COLS), jnp.float32),
             pltpu.SemaphoreType.DMA((DATES + 1,)),
         ],
-        compiler_params=pltpu.CompilerParams(vmem_limit_bytes=16 << 20),
+        compiler_params=pltpu.CompilerParams(vmem_limit_bytes=8 << 20),
         **kw,
-    )(factor, prediction, hindcast, truth, choices.T, filled[None])
+    )(
+        *(
+            pltpu.with_memory_space_constraint(x, pltpu.HBM)
+            for x in (factor, prediction, hindcast, truth, choices.T, filled[None])
+        )
+    )
 
 
 def lane_groups_sum(x):
@@ -116,14 +135,22 @@
 
 
 def column_kernel(got, out):
-    side0, pair0, truth0, num = got[:, 0], got[:, 1], got[:, 2], got[:, 3]
+    side0, pair0, truth0, mean = got[:, 0], got[:, 1], got[:, 2], got[:, 3]
     den, truth7, pair7, side7 = got[:, 4], got[:, 5], got[:, 6], got[:, 7]
+    dated0, dated7 = pair0 >= 0, pair7 >= 0
+    side0, pair0, pair7, side7 = (
+        jnp.sqrt(jnp.maximum(x, 0.0) * (1 / SQUARE_SCALE)) for x in (side0, pair0, pair7, side7)
+    )
+    truth0, truth7 = truth0 * (1 / TRUTH_SCALE), truth7 * (1 / TRUTH_SCALE)
+    den = jnp.where(den < 0, den * (-1 / SMALL_SCALE), den * (1 / LARGE_SCALE))
+    mean_size = jnp.sqrt(jnp.abs(mean) * (1 / MEAN_SCALE))
+    num = jnp.where(mean < 0, -mean_size, mean_size) * den
     band = lax.broadcasted_iota(jnp.int32, (TILES, LANES), 0)
     row = lax.broadcasted_iota(jnp.int32, (TILES, LANES), 1) // TW
     above = jnp.where(band == 0, 0.0, pltpu.roll(side7, 1, 0))
     below = jnp.where(band == TILES - 1, 0.0, pltpu.roll(side0, TILES - 1, 0))
-    weight0 = jnp.where(pair0 < 0, 0.0, fourth(pair0 + above))
-    weight7 = jnp.where(pair7 < 0, 0.0, fourth(pair7 + below))
+    weight0 = jnp.where(dated0, fourth(pair0 + above), 0.0)
+    weight7 = jnp.where(dated7, fourth(pair7 + below), 0.0)
     num = jnp.where(row == 0, lane_groups_sum(weight0 * truth0), num)
     num = jnp.where(row == ROWS - 1, lane_groups_sum(weight7 * truth7), num)
     den = jnp.where(row == 0, lane_groups_sum(weight0), den)
@@ -140,6 +167,7 @@
         out_shape=jax.ShapeDtypeStruct((8, 16, LANES), jnp.float32),
         in_specs=[vmem],
         out_specs=vmem,
+        compiler_params=pltpu.CompilerParams(vmem_limit_bytes=4 << 20),
         **kw,
     )(got)
 
@@ -168,6 +196,7 @@
         out_shape=jax.ShapeDtypeStruct((TW, 64), jnp.float32),
         in_specs=[vmem],
         out_specs=vmem,
+        compiler_params=pltpu.CompilerParams(vmem_limit_bytes=4 << 20),
         **kw,
     )(sums)
 
@@ -189,8 +218,9 @@
         tile_day_choices,
         filled_lengths,
     )
+    blocks = blocks.astype(jnp.float16)
     got = lax.all_to_all(blocks, "tile", split_axis=0, concat_axis=0, tiled=True)
-    sums = column_sums(got)
+    sums = column_sums(got.astype(jnp.float32))
     sums = lax.all_to_all(sums, "dgrp", split_axis=0, concat_axis=0, tiled=True)
     return analog_block(sums).T
 

time: 66 us -> 53.6 us (0.81)
  blocking collectives: 53.5 us -> 47.9 us
  local copies, waits for them, and re-layouts: 4.44 us -> 0 us
  Pallas kernels: 7.65 us -> 5.35 us
    all_to_all x1, blocking collectives: 40.3 us -> 35.1 us  [local(): lax.all_to_all(blocks, 'tile', split_axis=0, concat_axis=0, tiled=True)]
    unnamed x12 -> x0, local copies, waits for them, and re-layouts: 4.44 us -> none
    pallas_call x1, Pallas kernels: 1.99 us -> 0.81 us  [column_sums(): pl.pallas_call(column_kernel, out_shape=jax.ShapeDtypeStruct((8, 16, LANE...]
    pallas_call x1, Pallas kernels: 1.8 us -> 0.96 us  [analog_block(): pl.pallas_call(analog_kernel, out_shape=jax.ShapeDtypeStruct((TW, 64), jn...]
where the time goes in v2:
time: 53.6 us; the launch traced here: 53.4 us
  blocking collectives  47.9 us (89%)
  Pallas kernels  5.35 us (10%)
    all_to_all x1, blocking collectives, local(): lax.all_to_all(blocks, 'tile', split_axis=0, concat_axis=0, tiled=True)  35.1 us
    all_to_all x1, blocking collectives, local(): sums = lax.all_to_all(sums, 'dgrp', split_axis=0, concat_axis=0, tiled=True)  12.9 us
    pallas_call x1, Pallas kernels, band_blocks(): pl.pallas_call(functools.partial(band_kernel, first_date), out_shape=jax....  3.58 us

profile of v2, /device:TPU:1, one launch (start us, length us, event | category | flops | bytes accessed | tf_op | source)
XLA Modules:
  0.0 53.4 jit_solution(6346203272720716020)
XLA Ops:
  0.0 3.6 %shard_map.64 = f32[64,8,128]{2,1,0:T(8,128)S(1)} custom-call(f32[8]{0:T(128)} %factor.1, bf16[8,8,1024]{2,1,0:T(8,128)(2,1)} %pred_.1, bf16[8,8,8,1024]{3,2,1,0:T(8,128)(2,1)} %hind.1, bf16[8,8,1024]{2,1,0:T(8,128)(2,1)} %truth.1, s32[48,64]{1,0:T(8,128)} %bitcast.3, s32[1,64]{1,0:T(1,128)} %bitcast.4), custom_call_target="tpu_custom_call" | custom-call | tf_op jit(solution)/shard_map/pallas_call | solution.py:109
  3.6 35.1 %all_to_all.10 = f16[64,8,128]{2,1,0:T(8,128)(2,1)S(1)} all-to-all(f16[64,8,128]{2,1,0:T(8,128)(2,1)S(1)} %convert_element_type.6), channel_id=1, replica_groups=mesh['tile'=64,'dgrp'=8] {'tile'}, dimensions={0} | all-to-all | bytes 262144 | tf_op jit(solution)/shard_map/all_to_all | solution.py:222
  38.7 0.8 %shard_map.65 = f32[8,16,128]{2,1,0:T(8,128)S(1)} custom-call(f32[64,8,128]{2,1,0:T(8,128)S(1)} %convert_element_type.7.got), custom_call_target="tpu_custom_call" | custom-call | tf_op jit(solution)/shard_map/pallas_call | solution.py:165
  39.5 12.9 %all_to_all.11.sums = f32[8,16,128]{2,1,0:T(8,128)S(1)} all-to-all(f32[8,16,128]{2,1,0:T(8,128)S(1)} %shard_map.65), channel_id=1, replica_groups=mesh['tile'=64,'dgrp'=8] {'dgrp'}, dimensions={0} | all-to-all | bytes 131072 | tf_op jit(solution)/shard_map/all_to_all | solution.py:224
  52.4 1.0 %shard_map.66 = f32[16,64]{1,0:T(8,128)} custom-call(f32[8,16,128]{2,1,0:T(8,128)S(1)} %all_to_all.11.sums), custom_call_target="tpu_custom_call" | custom-call | tf_op jit(solution)/shard_map/pallas_call | solution.py:194
  (2 shorter events, 0.0 us)

commit v3 on v2

--- a/solution.py
+++ b/solution.py
@@ -10,6 +10,9 @@
 DATES, QTYS, ROWS, COLS = 8, 8, 8, 1024
 TILES, TW, LANES = 64, 16, 128
 MAXC = 48
+FIRST_TILE = 48
+TILE_ORDER = [(FIRST_TILE + i) % TILES for i in range(TILES)]
+GROUP_ORDER = [7, 6, 5, 4, 3, 2, 1, 0]
 GROUPS = LANES // TW
 
 SQUARE_SCALE, MEAN_SCALE, TRUTH_SCALE = 2.0**-7, 2.0**10, 2.0**13
@@ -30,7 +33,7 @@
 
 
 def fourth(dist9):
-    base = 1.0 / (1.0 + dist9 / 9.0)
+    base = 1.0 / (1.0 + dist9 * (1 / 9.0))
     base = base * base
     return base * base
 
@@ -41,18 +44,46 @@
 
 
 def band_kernel(
-    first_date, factor, pred, hind, truth, choices, filled, out, held, shown, exact, parts, sems
+    first_date,
+    factor_in,
+    pred_in,
+    hind_in,
+    truth_in,
+    choices_in,
+    filled_in,
+    out,
+    factor,
+    shown,
+    held,
+    truth,
+    choices,
+    filled,
+    exact,
+    parts,
+    sems,
 ):
-    copies = [pltpu.make_async_copy(hind.at[d], held.at[d], sems.at[d]) for d in range(DATES)]
-    seen = pltpu.make_async_copy(pred, shown, sems.at[DATES])
-    seen.start()
-    for copy in copies:
+    copies = [pltpu.make_async_copy(hind_in.at[d], held.at[d], sems.at[d]) for d in range(DATES)]
+    pairs = (
+        (choices_in, choices),
+        (filled_in, filled),
+        (pred_in, shown),
+        (factor_in, factor),
+        (truth_in, truth),
+    )
+    small = [
+        pltpu.make_async_copy(src, dst, sems.at[DATES + i]) for i, (src, dst) in enumerate(pairs)
+    ]
+    for copy in small[:4] + copies[:1] + small[4:] + copies[1:]:
         copy.start()
+    small[0].wait()
+    small[1].wait()
     member = member_rows(first_date(), choices[...], filled[...])
     col = lax.broadcasted_iota(jnp.int32, (ROWS, COLS), 1)
     sub = lax.broadcasted_iota(jnp.int32, (ROWS, COLS), 0)
-    seen.wait()
+    small[2].wait()
     exact[...] = shown[...].astype(jnp.float32)
+    small[3].wait()
+    small[4].wait()
     num = jnp.zeros((ROWS, COLS), jnp.float32)
     den = jnp.zeros((ROWS, COLS), jnp.float32)
     for d in range(DATES):
@@ -100,23 +131,26 @@
                 v[a] = jnp.where(odd, pltpu.roll(high, TW * s, 1), low)
                 v[a | s] = jnp.where(odd, high, pltpu.roll(low, LANES - TW * s, 1))
         for t in range(GROUPS):
-            out[j * GROUPS + t] = v[t]
+            out[(j * GROUPS + t - FIRST_TILE) % TILES] = v[t]
 
 
 def band_blocks(first_date, prediction, hindcast, truth, factor, choices, filled, **kw):
-    vmem = pl.BlockSpec(memory_space=pltpu.VMEM)
-    hbm = pl.BlockSpec(memory_space=pl.ANY)
+    hbm = pl.BlockSpec(memory_space=pltpu.HBM)
     return pl.pallas_call(
         functools.partial(band_kernel, first_date),
         out_shape=jax.ShapeDtypeStruct((TILES, ROWS, LANES), jnp.float32),
-        in_specs=[pl.BlockSpec(memory_space=pltpu.SMEM), hbm, hbm, vmem, vmem, vmem],
-        out_specs=vmem,
+        in_specs=[hbm] * 6,
+        out_specs=pl.BlockSpec(memory_space=pltpu.VMEM),
         scratch_shapes=[
+            pltpu.SMEM((QTYS,), jnp.float32),
+            pltpu.VMEM((QTYS, ROWS, COLS), jnp.bfloat16),
             pltpu.VMEM((DATES, QTYS, ROWS, COLS), jnp.bfloat16),
-            pltpu.VMEM((QTYS, ROWS, COLS), jnp.bfloat16),
+            pltpu.VMEM((DATES, ROWS, COLS), jnp.bfloat16),
+            pltpu.VMEM((MAXC, TILES), jnp.int32),
+            pltpu.VMEM((1, TILES), jnp.int32),
             pltpu.VMEM((QTYS, ROWS, COLS), jnp.float32),
             pltpu.VMEM((DATES, ROWS, COLS), jnp.float32),
-            pltpu.SemaphoreType.DMA((DATES + 1,)),
+            pltpu.SemaphoreType.DMA((DATES + 5,)),
         ],
         compiler_params=pltpu.CompilerParams(vmem_limit_bytes=8 << 20),
         **kw,
@@ -145,7 +179,7 @@
     den = jnp.where(den < 0, den * (-1 / SMALL_SCALE), den * (1 / LARGE_SCALE))
     mean_size = jnp.sqrt(jnp.abs(mean) * (1 / MEAN_SCALE))
     num = jnp.where(mean < 0, -mean_size, mean_size) * den
-    band = lax.broadcasted_iota(jnp.int32, (TILES, LANES), 0)
+    band = (lax.broadcasted_iota(jnp.int32, (TILES, LANES), 0) + FIRST_TILE) % TILES
     row = lax.broadcasted_iota(jnp.int32, (TILES, LANES), 1) // TW
     above = jnp.where(band == 0, 0.0, pltpu.roll(side7, 1, 0))
     below = jnp.where(band == TILES - 1, 0.0, pltpu.roll(side0, TILES - 1, 0))
@@ -155,9 +189,10 @@
     num = jnp.where(row == ROWS - 1, lane_groups_sum(weight7 * truth7), num)
     den = jnp.where(row == 0, lane_groups_sum(weight0), den)
     den = jnp.where(row == ROWS - 1, lane_groups_sum(weight7), den)
-    for g in range(8):
-        out[g, 0:8] = num[8 * g : 8 * g + 8]
-        out[g, 8:16] = den[8 * g : 8 * g + 8]
+    for place, g in enumerate(GROUP_ORDER):
+        at = (8 * g - FIRST_TILE) % TILES
+        out[place, 0:8] = num[at : at + 8]
+        out[place, 8:16] = den[at : at + 8]
 
 
 def column_sums(got, **kw):
@@ -219,9 +254,13 @@
         filled_lengths,
     )
     blocks = blocks.astype(jnp.float16)
-    got = lax.all_to_all(blocks, "tile", split_axis=0, concat_axis=0, tiled=True)
+    got = lax.all_to_all(
+        blocks, "tile", split_axis=0, concat_axis=0, tiled=True, axis_index_groups=[TILE_ORDER]
+    )
     sums = column_sums(got.astype(jnp.float32))
-    sums = lax.all_to_all(sums, "dgrp", split_axis=0, concat_axis=0, tiled=True)
+    sums = lax.all_to_all(
+        sums, "dgrp", split_axis=0, concat_axis=0, tiled=True, axis_index_groups=[GROUP_ORDER]
+    )
     return analog_block(sums).T
 
 

time: 53.6 us -> 43.7 us (0.82)
  blocking collectives: 47.9 us -> 38.6 us
  Pallas kernels: 5.35 us -> 4.52 us
    all_to_all x2, blocking collectives: 47.9 us -> 38.6 us  [the longest x1 28.2 us: local(): lax.all_to_all(blocks, 'tile', split_axis=0, concat_axis=0, tiled=True, a...]
    pallas_call x1, Pallas kernels: 3.58 us -> 2.76 us  [band_blocks(): pl.pallas_call(functools.partial(band_kernel, first_date), out_shape=jax....]
where the time goes in v3:
time: 43.7 us; the launch traced here: 43.2 us
  blocking collectives  38.6 us (88%)
  Pallas kernels  4.52 us (10%)
    all_to_all x1, blocking collectives, local(): lax.all_to_all(blocks, 'tile', split_axis=0, concat_axis=0, tiled=True, a...  28.2 us
    all_to_all x1, blocking collectives, local(): lax.all_to_all(sums, 'dgrp', split_axis=0, concat_axis=0, tiled=True, axi...  10.4 us
    pallas_call x1, Pallas kernels, band_blocks(): pl.pallas_call(functools.partial(band_kernel, first_date), out_shape=jax....  2.76 us
    pallas_call x1, Pallas kernels, analog_block(): pl.pallas_call(analog_kernel, out_shape=jax.ShapeDtypeStruct((TW, 64), jn...  0.96 us

profile of v3, /device:TPU:1, one launch (start us, length us, event | category | flops | bytes accessed | tf_op | source)
XLA Modules:
  0.0 43.2 jit_solution(16414115379265988229)
XLA Ops:
  0.0 2.8 %shard_map.64 = f32[64,8,128]{2,1,0:T(8,128)S(1)} custom-call(f32[8]{0:T(128)} %factor_in.1, bf16[8,8,1024]{2,1,0:T(8,128)(2,1)} %pred_in.1, bf16[8,8,8,1024]{3,2,1,0:T(8,128)(2,1)} %hind_in.1, bf16[8,8,1024]{2,1,0:T(8,128)(2,1)} %truth_in.1, s32[48,64]{1,0:T(8,128)} %bitcast.3, s32[1,64]{1,0:T(1,128)} %bitcast.4), custom_call_target="tpu_custom_call" | custom-call | tf_op jit(solution)/shard_map/pallas_call | solution.py:139
  2.8 28.2 %all_to_all.10 = f16[64,8,128]{2,1,0:T(8,128)(2,1)S(1)} all-to-all(f16[64,8,128]{2,1,0:T(8,128)(2,1)S(1)} %convert_element_type.6), channel_id=1, replica_groups={{384,392,400,408,416,424,432,440,448,456,464,472,480,488,496,504,0,8,16..., dimensions={0} | all-to-all | bytes 262144 | tf_op jit(solution)/shard_map/all_to_all | solution.py:257
  31.0 0.8 %shard_map.65 = f32[8,16,128]{2,1,0:T(8,128)S(1)} custom-call(f32[64,8,128]{2,1,0:T(8,128)S(1)} %convert_element_type.7.got), custom_call_target="tpu_custom_call" | custom-call | tf_op jit(solution)/shard_map/pallas_call | solution.py:200
  31.8 10.4 %all_to_all.11.sums = f32[8,16,128]{2,1,0:T(8,128)S(1)} all-to-all(f32[8,16,128]{2,1,0:T(8,128)S(1)} %shard_map.65), channel_id=1, replica_groups={{7,6,5,4,3,2,1,0},{15,14,13,12,11,10,9,8},{23,22,21,20,19,18,17,16},{31..., dimensions={0} | all-to-all | bytes 131072 | tf_op jit(solution)/shard_map/all_to_all | solution.py:261
  42.2 1.0 %shard_map.66 = f32[16,64]{1,0:T(8,128)} custom-call(f32[8,16,128]{2,1,0:T(8,128)S(1)} %all_to_all.11.sums), custom_call_target="tpu_custom_call" | custom-call | tf_op jit(solution)/shard_map/pallas_call | solution.py:229
  (2 shorter events, 0.0 us)

commit v4 on v3

--- a/solution.py
+++ b/solution.py
@@ -10,9 +10,10 @@
 DATES, QTYS, ROWS, COLS = 8, 8, 8, 1024
 TILES, TW, LANES = 64, 16, 128
 MAXC = 48
+WAITS = {0: (0, 1, 2), 3: (3, 4, 5, 6, 7)}
 FIRST_TILE = 48
 TILE_ORDER = [(FIRST_TILE + i) % TILES for i in range(TILES)]
-GROUP_ORDER = [7, 6, 5, 4, 3, 2, 1, 0]
+GROUP_ORDER = [6, 7, 5, 4, 3, 2, 1, 0]
 GROUPS = LANES // TW
 
 SQUARE_SCALE, MEAN_SCALE, TRUTH_SCALE = 2.0**-7, 2.0**10, 2.0**13
@@ -87,7 +88,8 @@
     num = jnp.zeros((ROWS, COLS), jnp.float32)
     den = jnp.zeros((ROWS, COLS), jnp.float32)
     for d in range(DATES):
-        copies[d].wait()
+        for later in WAITS.get(d, ()):
+            copies[later].wait()
         err = jnp.zeros((ROWS, COLS), jnp.float32)
         for v in range(QTYS):
             dev = exact[v] - held[d, v].astype(jnp.float32)
@@ -168,16 +170,40 @@
     return x
 
 
+def root(x):
+    x = jnp.maximum(x, 1e-30)
+    inverse = lax.rsqrt(x)
+    near = x * inverse
+    return near + 0.5 * inverse * (x - near * near)
+
+
+def rows_of_blocks(got):
+    sub = lax.broadcasted_iota(jnp.int32, (ROWS, LANES), 0)
+    rows = [[] for _ in range(ROWS)]
+    for g in range(TILES // ROWS):
+        v = [got[g * ROWS + i] for i in range(ROWS)]
+        for s in (1, 2, 4):
+            odd = (sub & s) != 0
+            for a in range(ROWS):
+                if a & s:
+                    continue
+                low, high = v[a], v[a | s]
+                v[a] = jnp.where(odd, pltpu.roll(high, s, 0), low)
+                v[a | s] = jnp.where(odd, high, pltpu.roll(low, ROWS - s, 0))
+        for k in range(ROWS):
+            rows[k].append(v[k])
+    return [jnp.concatenate(x, axis=0) for x in rows]
+
+
 def column_kernel(got, out):
-    side0, pair0, truth0, mean = got[:, 0], got[:, 1], got[:, 2], got[:, 3]
-    den, truth7, pair7, side7 = got[:, 4], got[:, 5], got[:, 6], got[:, 7]
+    side0, pair0, truth0, mean, den, truth7, pair7, side7 = rows_of_blocks(got)
     dated0, dated7 = pair0 >= 0, pair7 >= 0
     side0, pair0, pair7, side7 = (
-        jnp.sqrt(jnp.maximum(x, 0.0) * (1 / SQUARE_SCALE)) for x in (side0, pair0, pair7, side7)
+        root(x * (1 / SQUARE_SCALE)) for x in (side0, pair0, pair7, side7)
     )
     truth0, truth7 = truth0 * (1 / TRUTH_SCALE), truth7 * (1 / TRUTH_SCALE)
     den = jnp.where(den < 0, den * (-1 / SMALL_SCALE), den * (1 / LARGE_SCALE))
-    mean_size = jnp.sqrt(jnp.abs(mean) * (1 / MEAN_SCALE))
+    mean_size = root(jnp.abs(mean) * (1 / MEAN_SCALE))
     num = jnp.where(mean < 0, -mean_size, mean_size) * den
     band = (lax.broadcasted_iota(jnp.int32, (TILES, LANES), 0) + FIRST_TILE) % TILES
     row = lax.broadcasted_iota(jnp.int32, (TILES, LANES), 1) // TW

time: 43.7 us -> 42 us (0.961)
  Pallas kernels: 4.52 us -> 3.55 us
  blocking collectives: 38.6 us -> 37.8 us
    all_to_all x1, blocking collectives: 10.4 us -> 9.63 us  [local(): lax.all_to_all(sums, 'dgrp', split_axis=0, concat_axis=0, tiled=True, axi...]
    pallas_call x1, Pallas kernels: 2.76 us -> 2.25 us  [band_blocks(): pl.pallas_call(functools.partial(band_kernel, first_date), out_shape=jax....]
    pallas_call x1, Pallas kernels: 0.81 us -> 0.34 us  [column_sums(): pl.pallas_call(column_kernel, out_shape=jax.ShapeDtypeStruct((8, 16, LANE...]
where the time goes in v4:
time: 42 us; the launch traced here: 41.5 us
  blocking collectives  37.8 us (90%)
  Pallas kernels  3.55 us (8%)
    all_to_all x1, blocking collectives, local(): lax.all_to_all(blocks, 'tile', split_axis=0, concat_axis=0, tiled=True, a...  28.2 us
    all_to_all x1, blocking collectives, local(): lax.all_to_all(sums, 'dgrp', split_axis=0, concat_axis=0, tiled=True, axi...  9.63 us
    pallas_call x1, Pallas kernels, band_blocks(): pl.pallas_call(functools.partial(band_kernel, first_date), out_shape=jax....  2.25 us
    pallas_call x1, Pallas kernels, analog_block(): pl.pallas_call(analog_kernel, out_shape=jax.ShapeDtypeStruct((TW, 64), jn...  0.96 us

profile of v4, /device:TPU:1, one launch (start us, length us, event | category | flops | bytes accessed | tf_op | source)
XLA Modules:
  0.0 41.5 jit_solution(14173068543143373364)
XLA Ops:
  0.0 2.2 %shard_map.64 = f32[64,8,128]{2,1,0:T(8,128)S(1)} custom-call(f32[8]{0:T(128)} %factor_in.1, bf16[8,8,1024]{2,1,0:T(8,128)(2,1)} %pred_in.1, bf16[8,8,8,1024]{3,2,1,0:T(8,128)(2,1)} %hind_in.1, bf16[8,8,1024]{2,1,0:T(8,128)(2,1)} %truth_in.1, s32[48,64]{1,0:T(8,128)} %bitcast.3, s32[1,64]{1,0:T(1,128)} %bitcast.4), custom_call_target="tpu_custom_call" | custom-call | tf_op jit(solution)/shard_map/pallas_call | solution.py:141
  2.3 28.2 %all_to_all.10 = f16[64,8,128]{2,1,0:T(8,128)(2,1)S(1)} all-to-all(f16[64,8,128]{2,1,0:T(8,128)(2,1)S(1)} %convert_element_type.6), channel_id=1, replica_groups={{384,392,400,408,416,424,432,440,448,456,464,472,480,488,496,504,0,8,16..., dimensions={0} | all-to-all | bytes 262144 | tf_op jit(solution)/shard_map/all_to_all | solution.py:283
  30.5 0.3 shard_map.65
  30.9 9.6 %all_to_all.11.sums = f32[8,16,128]{2,1,0:T(8,128)S(1)} all-to-all(f32[8,16,128]{2,1,0:T(8,128)S(1)} %shard_map.65), channel_id=1, replica_groups={{6,7,5,4,3,2,1,0},{14,15,13,12,11,10,9,8},{22,23,21,20,19,18,17,16},{30..., dimensions={0} | all-to-all | bytes 131072 | tf_op jit(solution)/shard_map/all_to_all | solution.py:287
  40.5 1.0 %shard_map.66 = f32[16,64]{1,0:T(8,128)} custom-call(f32[8,16,128]{2,1,0:T(8,128)S(1)} %all_to_all.11.sums), custom_call_target="tpu_custom_call" | custom-call | tf_op jit(solution)/shard_map/pallas_call | solution.py:255
  (2 shorter events, 0.0 us)

commit v5 on v4

--- a/solution.py
+++ b/solution.py
@@ -17,6 +17,7 @@
 GROUPS = LANES // TW
 
 SQUARE_SCALE, MEAN_SCALE, TRUTH_SCALE = 2.0**-7, 2.0**10, 2.0**13
+SUM_SHIFT, MEAN_SHIFT = 2.0**-3, 2.0**-11
 SMALL, LARGE_SCALE, SMALL_SCALE = 2.0**-26, 2.0**12, 2.0**41
 
 
@@ -103,9 +104,9 @@
         weight = fourth(side + above + below) * flag
         num = num + weight * seen_truth
         den = den + weight
-        pair = jnp.where(sub == 1, side + above, side + below)
-        pair = jnp.where(flag > 0, pair * pair * SQUARE_SCALE, -1.0)
-        part = jnp.where((sub == 1) | (sub == 6), pair, side * side * SQUARE_SCALE)
+        part = jnp.where(sub == 1, side + above, jnp.where(sub == 6, side + below, side)) + SUM_SHIFT
+        part = part * part * SQUARE_SCALE
+        part = jnp.where(((sub == 1) | (sub == 6)) & (flag == 0), -1.0, part)
         scaled = seen_truth * TRUTH_SCALE
         part = jnp.where(sub == 2, pltpu.roll(scaled, 2, 0), part)
         parts[d] = jnp.where(sub == 5, pltpu.roll(scaled, ROWS - 2, 0), part)
@@ -113,7 +114,9 @@
     den = to_11_bits(jnp.where(high, den * LARGE_SCALE, den * -SMALL_SCALE))
     held_den = jnp.where(high, den * (1 / LARGE_SCALE), den * (-1 / SMALL_SCALE))
     mean = jnp.where(held_den > 0, num / held_den, 0.0)
-    num = mean * jnp.abs(mean) * MEAN_SCALE
+    size = jnp.abs(mean) + MEAN_SHIFT
+    size = size * size * MEAN_SCALE
+    num = jnp.where(mean < 0, -size, size)
     lane = lax.broadcasted_iota(jnp.int32, (ROWS, LANES), 1) // TW
     sub = lax.broadcasted_iota(jnp.int32, (ROWS, LANES), 0)
     for j in range(COLS // LANES):
@@ -199,11 +202,12 @@
     side0, pair0, truth0, mean, den, truth7, pair7, side7 = rows_of_blocks(got)
     dated0, dated7 = pair0 >= 0, pair7 >= 0
     side0, pair0, pair7, side7 = (
-        root(x * (1 / SQUARE_SCALE)) for x in (side0, pair0, pair7, side7)
+        jnp.maximum(root(x * (1 / SQUARE_SCALE)) - SUM_SHIFT, 0.0)
+        for x in (side0, pair0, pair7, side7)
     )
     truth0, truth7 = truth0 * (1 / TRUTH_SCALE), truth7 * (1 / TRUTH_SCALE)
     den = jnp.where(den < 0, den * (-1 / SMALL_SCALE), den * (1 / LARGE_SCALE))
-    mean_size = root(jnp.abs(mean) * (1 / MEAN_SCALE))
+    mean_size = root(jnp.abs(mean) * (1 / MEAN_SCALE)) - MEAN_SHIFT
     num = jnp.where(mean < 0, -mean_size, mean_size) * den
     band = (lax.broadcasted_iota(jnp.int32, (TILES, LANES), 0) + FIRST_TILE) % TILES
     row = lax.broadcasted_iota(jnp.int32, (TILES, LANES), 1) // TW
@@ -240,12 +244,10 @@
     analog = total[0:8] / total[8:16]
     lane = lax.broadcasted_iota(jnp.int32, (8, LANES), 1)
     sub = lax.broadcasted_iota(jnp.int32, (8, LANES), 0)
-    x = jnp.take_along_axis(analog, (lane % 8) * TW + lane // 8, axis=1)
-    for s in (1, 2, 4):
-        odd_lane, odd_sub = ((lane // 8) & s) != 0, (sub & s) != 0
-        up = pltpu.roll(pltpu.roll(x, 8 - s, 0), 8 * s, 1)
-        down = pltpu.roll(pltpu.roll(x, s, 0), LANES - 8 * s, 1)
-        x = jnp.where(odd_lane == odd_sub, x, jnp.where(odd_lane, up, down))
+    half, middle, row = lane // 64, lane // 8 % 8, lane % 8
+    x = jnp.take_along_axis(analog, row * TW + half * 8 + (middle + sub) % 8, axis=1)
+    x = jnp.take_along_axis(x, (sub - middle) % 8, axis=0)
+    x = jnp.take_along_axis(x, half * 64 + (sub - middle) % 8 * 8 + row, axis=1)
     out[0:8] = x[:, 0:64]
     out[8:16] = x[:, 64:128]
 

time: 42 us -> 41.9 us (level)
  no operation moved by 1% of the time
where the time goes in v5:
time: 41.9 us; the launch traced here: 41.4 us
  blocking collectives  37.8 us (90%)
  Pallas kernels  3.44 us (8%)
    all_to_all x1, blocking collectives, local(): lax.all_to_all(blocks, 'tile', split_axis=0, concat_axis=0, tiled=True, a...  28.2 us
    all_to_all x1, blocking collectives, local(): lax.all_to_all(sums, 'dgrp', split_axis=0, concat_axis=0, tiled=True, axi...  9.63 us
    pallas_call x1, Pallas kernels, band_blocks(): pl.pallas_call(functools.partial(band_kernel, first_date), out_shape=jax....  2.27 us

profile of v5, /device:TPU:1, one launch (start us, length us, event | category | flops | bytes accessed | tf_op | source)
XLA Modules:
  0.0 41.4 jit_solution(477389285756137511)
XLA Ops:
  0.0 2.3 %shard_map.64 = f32[64,8,128]{2,1,0:T(8,128)S(1)} custom-call(f32[8]{0:T(128)} %factor_in.1, bf16[8,8,1024]{2,1,0:T(8,128)(2,1)} %pred_in.1, bf16[8,8,8,1024]{3,2,1,0:T(8,128)(2,1)} %hind_in.1, bf16[8,8,1024]{2,1,0:T(8,128)(2,1)} %truth_in.1, s32[48,64]{1,0:T(8,128)} %bitcast.3, s32[1,64]{1,0:T(1,128)} %bitcast.4), custom_call_target="tpu_custom_call" | custom-call | tf_op jit(solution)/shard_map/pallas_call | solution.py:144
  2.3 28.2 %all_to_all.10 = f16[64,8,128]{2,1,0:T(8,128)(2,1)S(1)} all-to-all(f16[64,8,128]{2,1,0:T(8,128)(2,1)S(1)} %convert_element_type.6), channel_id=1, replica_groups={{384,392,400,408,416,424,432,440,448,456,464,472,480,488,496,504,0,8,16..., dimensions={0} | all-to-all | bytes 262144 | tf_op jit(solution)/shard_map/all_to_all | solution.py:285
  30.5 0.3 shard_map.65
  30.9 9.6 %all_to_all.11.sums = f32[8,16,128]{2,1,0:T(8,128)S(1)} all-to-all(f32[8,16,128]{2,1,0:T(8,128)S(1)} %shard_map.65), channel_id=1, replica_groups={{6,7,5,4,3,2,1,0},{14,15,13,12,11,10,9,8},{22,23,21,20,19,18,17,16},{30..., dimensions={0} | all-to-all | bytes 131072 | tf_op jit(solution)/shard_map/all_to_all | solution.py:289
  40.5 0.8 %shard_map.66 = f32[16,64]{1,0:T(8,128)} custom-call(f32[8,16,128]{2,1,0:T(8,128)S(1)} %all_to_all.11.sums), custom_call_target="tpu_custom_call" | custom-call | tf_op jit(solution)/shard_map/pallas_call | solution.py:257
  (2 shorter events, 0.0 us)

commit v6 on v5

--- a/solution.py
+++ b/solution.py
@@ -38,6 +38,17 @@
     base = 1.0 / (1.0 + dist9 * (1 / 9.0))
     base = base * base
     return base * base
+
+
+def turned(v, place, axis, step):
+    def moved(x, places):
+        return pltpu.roll(x, places % 8 * step, axis) if places % 8 else x
+
+    v = [moved(v[-i % 8], -i % 8) for i in range(8)]
+    for s in (1, 2, 4):
+        odd = (place & s) != 0
+        v = [jnp.where(odd, v[(i - s) % 8], v[i]) for i in range(8)]
+    return [moved(v[t], -t) for t in range(8)]
 
 
 def to_11_bits(x):
@@ -75,8 +86,17 @@
     small = [
         pltpu.make_async_copy(src, dst, sems.at[DATES + i]) for i, (src, dst) in enumerate(pairs)
     ]
-    for copy in small[:4] + copies[:1] + small[4:] + copies[1:]:
+    def start_date(d):
+        for v in range(0, QTYS, 2):
+            part = pl.ds(v, 2)
+            pltpu.make_async_copy(hind_in.at[d, part], held.at[d, part], sems.at[d]).start()
+
+    for copy in small[:4]:
         copy.start()
+    start_date(0)
+    small[4].start()
+    for d in range(1, DATES):
+        start_date(d)
     small[0].wait()
     small[1].wait()
     member = member_rows(first_date(), choices[...], filled[...])
@@ -127,14 +147,7 @@
             part = jnp.where(sub == 3, pltpu.roll(num[:, at], (3 - d) % ROWS, 0), part)
             part = jnp.where(sub == 4, pltpu.roll(den[:, at], (4 - d) % ROWS, 0), part)
             v.append(part)
-        for s in (1, 2, 4):
-            odd = (lane & s) != 0
-            for a in range(GROUPS):
-                if a & s:
-                    continue
-                low, high = v[a], v[a | s]
-                v[a] = jnp.where(odd, pltpu.roll(high, TW * s, 1), low)
-                v[a | s] = jnp.where(odd, high, pltpu.roll(low, LANES - TW * s, 1))
+        v = turned(v, lane, 1, TW)
         for t in range(GROUPS):
             out[(j * GROUPS + t - FIRST_TILE) % TILES] = v[t]
 
@@ -185,14 +198,7 @@
     rows = [[] for _ in range(ROWS)]
     for g in range(TILES // ROWS):
         v = [got[g * ROWS + i] for i in range(ROWS)]
-        for s in (1, 2, 4):
-            odd = (sub & s) != 0
-            for a in range(ROWS):
-                if a & s:
-                    continue
-                low, high = v[a], v[a | s]
-                v[a] = jnp.where(odd, pltpu.roll(high, s, 0), low)
-                v[a | s] = jnp.where(odd, high, pltpu.roll(low, ROWS - s, 0))
+        v = turned(v, sub, 0, 1)
         for k in range(ROWS):
             rows[k].append(v[k])
     return [jnp.concatenate(x, axis=0) for x in rows]

time: 41.9 us -> 41.7 us (level)
  no operation moved by 1% of the time
where the time goes in v6:
time: 41.7 us; the launch traced here: 41.2 us
  blocking collectives  37.8 us (91%)
  Pallas kernels  3.25 us (8%)
    all_to_all x1, blocking collectives, local(): lax.all_to_all(blocks, 'tile', split_axis=0, concat_axis=0, tiled=True, a...  28.2 us
    all_to_all x1, blocking collectives, local(): lax.all_to_all(sums, 'dgrp', split_axis=0, concat_axis=0, tiled=True, axi...  9.63 us
    pallas_call x1, Pallas kernels, band_blocks(): pl.pallas_call(functools.partial(band_kernel, first_date), out_shape=jax....  2.08 us

profile of v6, /device:TPU:1, one launch (start us, length us, event | category | flops | bytes accessed | tf_op | source)
XLA Modules:
  0.0 41.2 jit_solution(17476845235534545347)
XLA Ops:
  0.0 2.1 %shard_map.64 = f32[64,8,128]{2,1,0:T(8,128)S(1)} custom-call(f32[8]{0:T(128)} %factor_in.1, bf16[8,8,1024]{2,1,0:T(8,128)(2,1)} %pred_in.1, bf16[8,8,8,1024]{3,2,1,0:T(8,128)(2,1)} %hind_in.1, bf16[8,8,1024]{2,1,0:T(8,128)(2,1)} %truth_in.1, s32[48,64]{1,0:T(8,128)} %bitcast.3, s32[1,64]{1,0:T(1,128)} %bitcast.4), custom_call_target="tpu_custom_call" | custom-call | tf_op jit(solution)/shard_map/pallas_call | solution.py:157
  2.1 28.2 %all_to_all.10 = f16[64,8,128]{2,1,0:T(8,128)(2,1)S(1)} all-to-all(f16[64,8,128]{2,1,0:T(8,128)(2,1)S(1)} %convert_element_type.6), channel_id=1, replica_groups={{384,392,400,408,416,424,432,440,448,456,464,472,480,488,496,504,0,8,16..., dimensions={0} | all-to-all | bytes 262144 | tf_op jit(solution)/shard_map/all_to_all | solution.py:291
  30.4 0.3 shard_map.65
  30.7 9.6 %all_to_all.11.sums = f32[8,16,128]{2,1,0:T(8,128)S(1)} all-to-all(f32[8,16,128]{2,1,0:T(8,128)S(1)} %shard_map.65), channel_id=1, replica_groups={{6,7,5,4,3,2,1,0},{14,15,13,12,11,10,9,8},{22,23,21,20,19,18,17,16},{30..., dimensions={0} | all-to-all | bytes 131072 | tf_op jit(solution)/shard_map/all_to_all | solution.py:295
  40.3 0.8 %shard_map.66 = f32[16,64]{1,0:T(8,128)} custom-call(f32[8,16,128]{2,1,0:T(8,128)S(1)} %all_to_all.11.sums), custom_call_target="tpu_custom_call" | custom-call | tf_op jit(solution)/shard_map/pallas_call | solution.py:263
  (2 shorter events, 0.0 us)

commit v7 on v6

--- a/solution.py
+++ b/solution.py
@@ -91,8 +91,11 @@
             part = pl.ds(v, 2)
             pltpu.make_async_copy(hind_in.at[d, part], held.at[d, part], sems.at[d]).start()
 
-    for copy in small[:4]:
+    for copy in small[:2] + small[3:4]:
         copy.start()
+    for v in range(0, QTYS, 2):
+        part = pl.ds(v, 2)
+        pltpu.make_async_copy(pred_in.at[part], shown.at[part], sems.at[DATES + 2]).start()
     start_date(0)
     small[4].start()
     for d in range(1, DATES):

time: 41.7 us -> 41.7 us (level)
  no operation moved by 1% of the time
where the time goes in v7:
time: 41.7 us; the launch traced here: 41.2 us
  blocking collectives  37.8 us (91%)
  Pallas kernels  3.27 us (8%)
    all_to_all x1, blocking collectives, local(): lax.all_to_all(blocks, 'tile', split_axis=0, concat_axis=0, tiled=True, a...  28.2 us
    all_to_all x1, blocking collectives, local(): lax.all_to_all(sums, 'dgrp', split_axis=0, concat_axis=0, tiled=True, axi...  9.63 us
    pallas_call x1, Pallas kernels, band_blocks(): pl.pallas_call(functools.partial(band_kernel, first_date), out_shape=jax....  2.1 us

profile of v7, /device:TPU:1, one launch (start us, length us, event | category | flops | bytes accessed | tf_op | source)
XLA Modules:
  0.0 41.2 jit_solution(17515494252957140635)
XLA Ops:
  0.0 2.1 %shard_map.64 = f32[64,8,128]{2,1,0:T(8,128)S(1)} custom-call(f32[8]{0:T(128)} %factor_in.1, bf16[8,8,1024]{2,1,0:T(8,128)(2,1)} %pred_in.1, bf16[8,8,8,1024]{3,2,1,0:T(8,128)(2,1)} %hind_in.1, bf16[8,8,1024]{2,1,0:T(8,128)(2,1)} %truth_in.1, s32[48,64]{1,0:T(8,128)} %bitcast.3, s32[1,64]{1,0:T(1,128)} %bitcast.4), custom_call_target="tpu_custom_call" | custom-call | tf_op jit(solution)/shard_map/pallas_call | solution.py:160
  2.1 28.2 %all_to_all.10 = f16[64,8,128]{2,1,0:T(8,128)(2,1)S(1)} all-to-all(f16[64,8,128]{2,1,0:T(8,128)(2,1)S(1)} %convert_element_type.6), channel_id=1, replica_groups={{384,392,400,408,416,424,432,440,448,456,464,472,480,488,496,504,0,8,16..., dimensions={0} | all-to-all | bytes 262144 | tf_op jit(solution)/shard_map/all_to_all | solution.py:294
  30.4 0.3 shard_map.65
  30.7 9.6 %all_to_all.11.sums = f32[8,16,128]{2,1,0:T(8,128)S(1)} all-to-all(f32[8,16,128]{2,1,0:T(8,128)S(1)} %shard_map.65), channel_id=1, replica_groups={{6,7,5,4,3,2,1,0},{14,15,13,12,11,10,9,8},{22,23,21,20,19,18,17,16},{30..., dimensions={0} | all-to-all | bytes 131072 | tf_op jit(solution)/shard_map/all_to_all | solution.py:298
  40.3 0.8 %shard_map.66 = f32[16,64]{1,0:T(8,128)} custom-call(f32[8,16,128]{2,1,0:T(8,128)S(1)} %all_to_all.11.sums), custom_call_target="tpu_custom_call" | custom-call | tf_op jit(solution)/shard_map/pallas_call | solution.py:266
  (2 shorter events, 0.0 us)

commit v8 on v7

--- a/solution.py
+++ b/solution.py
@@ -13,7 +13,7 @@
 WAITS = {0: (0, 1, 2), 3: (3, 4, 5, 6, 7)}
 FIRST_TILE = 48
 TILE_ORDER = [(FIRST_TILE + i) % TILES for i in range(TILES)]
-GROUP_ORDER = [6, 7, 5, 4, 3, 2, 1, 0]
+GROUP_ORDER = [7, 6, 5, 4, 3, 2, 1, 0]
 GROUPS = LANES // TW
 
 SQUARE_SCALE, MEAN_SCALE, TRUTH_SCALE = 2.0**-7, 2.0**10, 2.0**13

time: 41.7 us -> 42.5 us (1.019)
  blocking collectives: 37.8 us -> 38.6 us
    all_to_all x1, blocking collectives: 9.63 us -> 10.4 us  [local(): lax.all_to_all(sums, 'dgrp', split_axis=0, concat_axis=0, tiled=True, axi...]
where the time goes in v8:
time: 42.5 us; the launch traced here: 41.9 us
  blocking collectives  38.6 us (91%)
  Pallas kernels  3.27 us (8%)
    all_to_all x1, blocking collectives, local(): lax.all_to_all(blocks, 'tile', split_axis=0, concat_axis=0, tiled=True, a...  28.2 us
    all_to_all x1, blocking collectives, local(): lax.all_to_all(sums, 'dgrp', split_axis=0, concat_axis=0, tiled=True, axi...  10.4 us
    pallas_call x1, Pallas kernels, band_blocks(): pl.pallas_call(functools.partial(band_kernel, first_date), out_shape=jax....  2.1 us

profile of v8, /device:TPU:1, one launch (start us, length us, event | category | flops | bytes accessed | tf_op | source)
XLA Modules:
  0.0 41.9 jit_solution(9103110053910235088)
XLA Ops:
  0.0 2.1 %shard_map.64 = f32[64,8,128]{2,1,0:T(8,128)S(1)} custom-call(f32[8]{0:T(128)} %factor_in.1, bf16[8,8,1024]{2,1,0:T(8,128)(2,1)} %pred_in.1, bf16[8,8,8,1024]{3,2,1,0:T(8,128)(2,1)} %hind_in.1, bf16[8,8,1024]{2,1,0:T(8,128)(2,1)} %truth_in.1, s32[48,64]{1,0:T(8,128)} %bitcast.3, s32[1,64]{1,0:T(1,128)} %bitcast.4), custom_call_target="tpu_custom_call" | custom-call | tf_op jit(solution)/shard_map/pallas_call | solution.py:160
  2.1 28.2 %all_to_all.10 = f16[64,8,128]{2,1,0:T(8,128)(2,1)S(1)} all-to-all(f16[64,8,128]{2,1,0:T(8,128)(2,1)S(1)} %convert_element_type.6), channel_id=1, replica_groups={{384,392,400,408,416,424,432,440,448,456,464,472,480,488,496,504,0,8,16..., dimensions={0} | all-to-all | bytes 262144 | tf_op jit(solution)/shard_map/all_to_all | solution.py:294
  30.4 0.3 shard_map.65
  30.7 10.4 %all_to_all.11.sums = f32[8,16,128]{2,1,0:T(8,128)S(1)} all-to-all(f32[8,16,128]{2,1,0:T(8,128)S(1)} %shard_map.65), channel_id=1, replica_groups={{7,6,5,4,3,2,1,0},{15,14,13,12,11,10,9,8},{23,22,21,20,19,18,17,16},{31..., dimensions={0} | all-to-all | bytes 131072 | tf_op jit(solution)/shard_map/all_to_all | solution.py:298
  41.1 0.8 %shard_map.66 = f32[16,64]{1,0:T(8,128)} custom-call(f32[8,16,128]{2,1,0:T(8,128)S(1)} %all_to_all.11.sums), custom_call_target="tpu_custom_call" | custom-call | tf_op jit(solution)/shard_map/pallas_call | solution.py:266
  (2 shorter events, 0.0 us)
